TPU v7x, 32 devices: a whole 2x2x4 slice. The times are simulated.
32 devices in a mesh: groups: 2 (over x), pool: 2 (over core), tensor: 8 (over z, y).
Axes of the slice: x: 2, y: 2, z: 4, core: 2. Of those that a mesh axis runs over, the one named last changes fastest.
Arguments:
- rows: bfloat16 [512, 8192], P(('groups', 'pool', 'tensor')), parts along dimension 0, may hold values from -6 to 6
- norm_gain: float32 [8192], replicated, may hold values from 0.1 to 1.9
- w_query: bfloat16 [8192, 8192], P(None, ('pool', 'tensor')), may hold values from -0.0625 to 0.0625
- w_keyval: bfloat16 [8192, 2048], P(None, ('pool', 'tensor')), may hold values from -0.125 to 0.125
- w_out: bfloat16 [8192, 8192], P(('pool', 'tensor')), may hold values from -0.25 to 0.25
- key_cache: bfloat16 [512, 256, 1024], P(('groups', 'pool', 'tensor')), parts along dimension 0, may hold values from -104 to 104
- value_cache: bfloat16 [512, 256, 1024], P(('groups', 'pool', 'tensor')), parts along dimension 0, may hold values from -6 to 6
- lengths: int32 [512], P('groups'), parts along dimension 0, may hold values from 1 to 256, as said below
- slot_of: int32 [512], P('groups'), parts along dimension 0, may hold values from 0 to 255, each once
Outputs:
- projected: bfloat16 [512, 8192], P(('groups', 'pool', 'tensor')), parts along dimension 0
There are 2 independent parts, one for each index of `groups`. A program takes and returns all parts, laid end to end along the dimension named above; an argument that names none is the same for every part. Nothing has to cross between parts.
Inputs may be any that keep to these rules, and one draw needn't show every extreme that they name: `slot_of`: slots 16 * i to 16 * (i + 1) - 1 lie on index i of pool+tensor; every slot belongs to exactly one request. `lengths`: some request has exactly 256 cached tokens.
All inputs are finite; a program needn't handle non-finite values.
Results may differ from a plain program's by a relative error of at most 0.024.
Values may be sent and summed in bfloat16 or wider, within the bound.
A program may use at most 128 MiB of HBM per device.

v0:
```python
import jax
import jax.numpy as jnp
from jax import lax
from jax.sharding import PartitionSpec as P

HEADS = 64
KVH = 8
HD = 128
L = 256


EPS = 1e-05


def body(rows, norm_gain, w_query, w_keyval, w_out, key_cache, value_cache, lengths, slot_of):
    devices = lax.axis_size(("pool", "tensor"))
    slots_dev = key_cache.shape[0]
    requests = slots_dev * devices
    query_cols = w_query.shape[1]
    width = query_cols + w_keyval.shape[1]
    group = HEADS // KVH
    scale = HD ** (-0.5)
    block = min(L, 128)
    values32 = lax.all_gather(rows, ("pool", "tensor"), axis=0, tiled=True).astype(jnp.float32)
    normed = (
        values32 * lax.rsqrt(jnp.mean(values32 * values32, axis=1, keepdims=True) + EPS) * norm_gain
    ).astype(jnp.bfloat16)
    queries = jnp.dot(normed, w_query, preferred_element_type=jnp.float32).astype(jnp.bfloat16)
    keyvals = jnp.dot(normed, w_keyval, preferred_element_type=jnp.float32).astype(jnp.bfloat16)
    projected_cols = jnp.concatenate([queries, keyvals], axis=1)
    slot_ids = jnp.arange(requests, dtype=jnp.int32)
    sort_map = (slot_of[None, :] == slot_ids[:, None]).astype(jnp.bfloat16)
    in_slots = jnp.dot(sort_map, projected_cols, preferred_element_type=jnp.float32).astype(
        jnp.bfloat16
    )
    arrived = lax.all_to_all(
        in_slots.reshape(requests, 1, width),
        ("pool", "tensor"),
        split_axis=0,
        concat_axis=1,
        tiled=True,
    )
    query = arrived[:, :, :query_cols].reshape(slots_dev, KVH, group, HD)
    keyval = arrived[:, :, query_cols:].reshape(slots_dev, 2, KVH, HD)
    new_keys = keyval[:, 0]
    new_values = keyval[:, 1]
    first_slot = lax.axis_index(("pool", "tensor")) * slots_dev
    own_slots = first_slot + jnp.arange(slots_dev, dtype=jnp.int32)
    slot_len = jnp.sum(
        jnp.where(slot_of[None, :] == own_slots[:, None], lengths[None, :], 0), axis=1
    )
    own_scores = (
        jnp.einsum("skgd,skd->skg", query, new_keys, preferred_element_type=jnp.float32) * scale
    )
    start_state = (
        own_scores,
        jnp.ones_like(own_scores),
        jnp.broadcast_to(
            new_values.astype(jnp.float32)[:, :, None, :], (slots_dev, KVH, group, HD)
        ),
    )

    def visit(block_idx, state):
        running, totals, weighted = state
        begin = block_idx * block
        keys_blk = lax.dynamic_slice_in_dim(key_cache, begin, block, 1).reshape(
            slots_dev, block, KVH, HD
        )
        values_blk = lax.dynamic_slice_in_dim(value_cache, begin, block, 1).reshape(
            slots_dev, block, KVH, HD
        )
        scores = (
            jnp.einsum("skgd,slkd->skgl", query, keys_blk, preferred_element_type=jnp.float32)
            * scale
        )
        live = (begin + jnp.arange(block, dtype=jnp.int32))[None, :] < slot_len[:, None]
        scores = jnp.where(live[:, None, None, :], scores, -1e30)
        newest = jnp.maximum(running, jnp.max(scores, axis=3))
        probs = jnp.exp(scores - newest[..., None])
        shrink = jnp.exp(running - newest)
        totals = totals * shrink + jnp.sum(probs, axis=3)
        weighted = weighted * shrink[..., None] + jnp.einsum(
            "skgl,slkd->skgd",
            probs.astype(jnp.bfloat16),
            values_blk,
            preferred_element_type=jnp.float32,
        )
        return (newest, totals, weighted)

    block_count = L // block
    running, totals, weighted = lax.fori_loop(0, block_count, visit, start_state)
    attended = (weighted / totals[..., None]).astype(jnp.bfloat16).reshape(slots_dev, HEADS * HD)
    piece_cols = HEADS * HD // devices
    positions = jnp.arange(requests, dtype=jnp.int32)
    returned = lax.all_to_all(
        attended.reshape(slots_dev, devices, piece_cols),
        ("pool", "tensor"),
        split_axis=1,
        concat_axis=0,
        tiled=True,
    )
    returned = returned.reshape(requests, piece_cols)
    back_map = (slot_of[:, None] == positions[None, :]).astype(jnp.bfloat16)
    in_requests = jnp.dot(back_map, returned, preferred_element_type=jnp.float32).astype(
        jnp.bfloat16
    )
    return lax.psum_scatter(
        jnp.dot(in_requests, w_out, preferred_element_type=jnp.float32).astype(jnp.bfloat16),
        ("pool", "tensor"),
        scatter_dimension=0,
        tiled=True,
    )


def solution(mesh):
    placed = (
        P(("groups", "pool", "tensor"), None),
        P(),
        P(None, ("pool", "tensor")),
        P(None, ("pool", "tensor")),
        P(("pool", "tensor"), None),
        P(("groups", "pool", "tensor"), None, None),
        P(("groups", "pool", "tensor"), None, None),
        P("groups"),
        P("groups"),
    )
    return jax.shard_map(
        body,
        mesh=mesh,
        in_specs=placed,
        out_specs=P(("groups", "pool", "tensor"), None),
        check_vma=False,
    )
```

profile of v0, /device:TPU:0, one launch (start us, length us, event | category | flops | bytes accessed | tf_op | source)
XLA Modules:
  0.0 250.2 jit_solution(16815218170721360737)
XLA Ops:
  6.5 0.0 copy-start
  6.5 0.0 copy-start.5
  6.5 0.0 all-gather.2.cloned.1.call-start
  6.5 0.7 all-gather.2.cloned.1.call-update
  7.3 55.6 %all-gather.2.cloned.1.call-done = bf16[256,8192]{1,0:T(8,128)(2,1)} async-done(((bf16[16,8192]{1,0:T(8,128)(2,1)}), bf16[256,8192]{1,0:T(8,128)(2,1)}) %all-gather.2.cloned.1.call-update) | async-done | bytes 4194320 | tf_op jit(solution)/shard_map/all_gather | solution.py:24
  62.9 0.0 copy-start.2
  62.9 3.3 %fusion.7 = f32[256]{0:T(256)S(1)} fusion(bf16[256,8192]{1,0:T(8,128)(2,1)} %all-gather.2.cloned.1.call-done), kind=kLoop, calls=%fused_computation.18 | loop fusion | flops 6291200 | bytes 4195328 | tf_op jit(solution)/shard_map/reduce_sum | solution.py:26
  66.1 0.0 copy-done.5
  66.1 0.2 copy-done.2
  66.3 5.8 %convolution_convert_fusion.3 = bf16[256,512]{1,0:T(8,128)(2,1)S(1)} fusion(bf16[8192,512]{1,0:T(8,128)(2,1)} %param.13, bf16[256,8192]{1,0:T(8,128)(2,1)S(1)} %copy-done.2, f32[8192]{0:T(1024)S(1)} %copy-done.5, f32[256]{0:T(256)S(1)} %add_rsqrt_fusion), kind=kOutput, calls=%fused_computation.23 | convolution fusion | flops 2156003328 | bytes 12878848 | tf_op jit(solution)/shard_map/dot_general | solution.py:28
  72.1 0.0 copy-done
  72.2 0.0 copy-start.3
  72.2 0.0 copy-start.4
  72.2 1.5 fusion.14
  73.7 0.0 copy-done.3
  73.7 0.3 fusion.13
  74.0 0.5 broadcast.67
  74.5 0.8 reduce
  75.3 0.8 reshape.91
  76.1 3.5 %all-to-all-start = ((bf16[16,2,5120]{2,1,0:T(2,128)(2,1)}), bf16[16,2,5120]{2,1,0:T(2,128)(2,1)S(1)}, u32[]{:S(2)}, u32[]{:S(2)}) async-start(bf16[16,2,5120]{2,1,0:T(2,128)(2,1)} %reshape.91), calls=%async_computation | async-start | bytes 655360 | tf_op jit(solution)/shard_map/all_to_all | solution.py:36
  79.7 0.0 reduce-scatter.2.cloned.1.call-start
  79.7 0.0 copy-done.4
  79.8 0.2 select_reduce_fusion
  79.9 11.4 %all-to-all-done = bf16[16,2,5120]{2,1,0:T(2,128)(2,1)S(1)} async-done(((bf16[16,2,5120]{2,1,0:T(2,128)(2,1)}), bf16[16,2,5120]{2,1,0:T(2,128)(2,1)S(1)}, u32[]{:S(2)}, u32[]{:S(2)}) %all-to-all-start) | async-done | bytes 327712 | tf_op jit(solution)/shard_map/all_to_all | solution.py:36
  91.3 0.3 reshape.92
  91.7 0.2 copy.56
  91.8 0.2 reshape.83
  92.0 0.3 fusion.23
  92.4 59.2 %while.18 = (s32[]{:T(128)}, f32[16,8,8]{2,1,0:T(8,128)S(1)}, f32[16,8,8]{2,1,0:T(8,128)S(1)}, f32[16,8,8,128]{3,2,1,0:T(8,128)S(1)}, s32[16]{0:T(128)S(1)}, /*i...) while((s32[]{:T(128)}, f32[16,8,8]{2,1,0:T(8,128)S(1)}, ...), condition=%wide.region_5.6_spmd.clone, body=%wide.region_2.5_spmd.clone.sunk | while | flops 68293760 | bytes 44897524 | solution.py:91
  92.4 8.3 %constant_dynamic-slice_fusion.3 = (bf16[16,128,1024]{2,1,0:T(8,128)(2,1)}, bf16[16,128,1024]{2,1,0:T(8,128)(2,1)}) fusion(bf16[16,256,1024]{2,1,0:T(8,128)(2,1)} %get-tuple-element.338, s32[]{:T(128)S(6)} %select_n.32, bf16[16,256,1024]{2,1,0:T(8,128)(2,1)} %get-tuple-element.336), kind=kLoop, calls=%fused_computation.12.clone.1 | loop fusion | bytes 16777220 | tf_op jit(solution)/shard_map/while/body/eval_jaxpr/dynamic_slice | solution.py:69
  100.7 6.3 %copy.74 = bf16[16,128,1024]{1,2,0:T(8,128)(2,1)} copy(bf16[16,128,1024]{2,1,0:T(8,128)(2,1)} %get-tuple-element.301) | data formatting | bytes 8388608 | tf_op jit(solution)/shard_map/while/body/eval_jaxpr/dynamic_slice | solution.py:66
  107.1 0.1 broadcast_compare_fusion.2
  107.1 3.5 %fusion.47 = (f32[16,8,8]{2,1,0:T(8,128)S(1)}, f32[16,8,8,128]{3,2,1,0:T(8,128)S(1)}) fusion(bf16[16,128,8,128]{1,3,2,0:T(8,128)(2,1)} %bitcast.47, bf16[16,8,8,128]{3,2,1,0:T(8,128)(2,1)S(1)} %get-tuple-element.337, pred[16,128]{1,0:T(8,128)(4,1)S(1)} %broadcast_compare_fusion.2), kind=kOutput, calls=%fused_computation.45.clone.1 | convolution fusion | flops 33946624 | bytes 4986880 | tf_op jit(solution)/shard_map/while/body/eval_jaxpr/skgd,slkd->skgl/dot_general | solution.py:73
  110.6 0.4 fusion.48
  111.1 6.4 %copy.75 = bf16[16,128,1024]{1,2,0:T(8,128)(2,1)} copy(bf16[16,128,1024]{2,1,0:T(8,128)(2,1)} %get-tuple-element.305) | data formatting | bytes 8388608 | tf_op jit(solution)/shard_map/while/body/eval_jaxpr/dynamic_slice | solution.py:69
  117.5 4.5 %convolution_add_fusion.2 = f32[16,8,8,128]{3,2,1,0:T(8,128)S(1)} fusion(bf16[16,128,8,128]{1,3,2,0:T(8,128)(2,1)} %bitcast.48, f32[16,8,8,128]{3,2,1,0:T(8,128)S(1)} %get-tuple-element.322, f32[16,8,8,128]{3,2,1,0:T(8,128)S(1)} %get-tuple-element.303, f32[16,8,8]{2,1,0:T(8,128)S(1)} %get-tuple-element.306, f32[16,8,8]{2,1,0:T(8,128)S(1)} %max.9), kind=kOutput, calls=%fused_computation.clone.1 | convolution fusion | flops 34078720 | bytes 5775360 | tf_op jit(solution)/shard_map/while/body/eval_jaxpr/skgl,slkd->skgd/dot_general | solution.py:82
  122.0 8.3 %constant_dynamic-slice_fusion.3 = (bf16[16,128,1024]{2,1,0:T(8,128)(2,1)}, bf16[16,128,1024]{2,1,0:T(8,128)(2,1)}) fusion(bf16[16,256,1024]{2,1,0:T(8,128)(2,1)} %get-tuple-element.338, s32[]{:T(128)S(6)} %select_n.32, bf16[16,256,1024]{2,1,0:T(8,128)(2,1)} %get-tuple-element.336), kind=kLoop, calls=%fused_computation.12.clone.1 | loop fusion | bytes 16777220 | tf_op jit(solution)/shard_map/while/body/eval_jaxpr/dynamic_slice | solution.py:69
  130.3 6.3 %copy.74 = bf16[16,128,1024]{1,2,0:T(8,128)(2,1)} copy(bf16[16,128,1024]{2,1,0:T(8,128)(2,1)} %get-tuple-element.301) | data formatting | bytes 8388608 | tf_op jit(solution)/shard_map/while/body/eval_jaxpr/dynamic_slice | solution.py:66
  136.6 0.1 broadcast_compare_fusion.2
  136.7 3.5 %fusion.47 = (f32[16,8,8]{2,1,0:T(8,128)S(1)}, f32[16,8,8,128]{3,2,1,0:T(8,128)S(1)}) fusion(bf16[16,128,8,128]{1,3,2,0:T(8,128)(2,1)} %bitcast.47, bf16[16,8,8,128]{3,2,1,0:T(8,128)(2,1)S(1)} %get-tuple-element.337, pred[16,128]{1,0:T(8,128)(4,1)S(1)} %broadcast_compare_fusion.2), kind=kOutput, calls=%fused_computation.45.clone.1 | convolution fusion | flops 33946624 | bytes 4986880 | tf_op jit(solution)/shard_map/while/body/eval_jaxpr/skgd,slkd->skgl/dot_general | solution.py:73
  140.2 0.4 fusion.48
  140.7 6.4 %copy.75 = bf16[16,128,1024]{1,2,0:T(8,128)(2,1)} copy(bf16[16,128,1024]{2,1,0:T(8,128)(2,1)} %get-tuple-element.305) | data formatting | bytes 8388608 | tf_op jit(solution)/shard_map/while/body/eval_jaxpr/dynamic_slice | solution.py:69
  147.1 4.5 %convolution_add_fusion.2 = f32[16,8,8,128]{3,2,1,0:T(8,128)S(1)} fusion(bf16[16,128,8,128]{1,3,2,0:T(8,128)(2,1)} %bitcast.48, f32[16,8,8,128]{3,2,1,0:T(8,128)S(1)} %get-tuple-element.322, f32[16,8,8,128]{3,2,1,0:T(8,128)S(1)} %get-tuple-element.303, f32[16,8,8]{2,1,0:T(8,128)S(1)} %get-tuple-element.306, f32[16,8,8]{2,1,0:T(8,128)S(1)} %max.9), kind=kOutput, calls=%fused_computation.clone.1 | convolution fusion | flops 34078720 | bytes 5775360 | tf_op jit(solution)/shard_map/while/body/eval_jaxpr/skgl,slkd->skgd/dot_general | solution.py:82
  151.6 0.2 divide_convert_fusion
  151.8 0.2 reshape_reshape.3
  152.0 0.2 copy.60
  152.1 12.9 %all_to_all.33 = bf16[16,16,512]{2,0,1:T(8,128)(2,1)S(1)} all-to-all(bf16[16,16,512]{2,0,1:T(8,128)(2,1)S(1)} %copy.60), channel_id=1, replica_groups=mesh['groups'=2,'pool'=2,'tensor'=8] {'pool','tensor'}, dimensions={1} | all-to-all | bytes 524288 | tf_op jit(solution)/shard_map/all_to_all | solution.py:95
  165.1 0.0 copy-start.1
  165.1 8.0 %convolution_convert_fusion = bf16[256,8192]{1,0:T(8,128)(2,1)} fusion(bf16[512,8192]{1,0:T(8,128)(2,1)} %param.15, bf16[256,512]{1,0:T(8,128)(2,1)S(1)} %bitcast.49, s32[256]{0:T(256)S(1)} %copy-done.3), kind=kOutput, calls=%fused_computation.17 | convolution fusion | flops 2216886272 | bytes 12846080 | tf_op jit(solution)/shard_map/dot_general | solution.py:108
  173.0 0.0 reduce-scatter.2.cloned.1.call-update
  173.1 70.3 %reduce-scatter.2.cloned.1.call-done = bf16[16,8192]{1,0:T(8,128)(2,1)} async-done(((bf16[256,8192]{1,0:T(8,128)(2,1)}), bf16[16,8192]{1,0:T(8,128)(2,1)}) %reduce-scatter.2.cloned.1.call-update) | async-done | bytes 262160 | tf_op jit(solution)/shard_map/reduce_scatter | solution.py:107
  243.4 0.0 copy-done.1
  (18 shorter events, 0.3 us)
Async XLA Ops:
  6.5 65.6 %copy-start = (bf16[8192,128]{1,0:T(8,128)(2,1)S(1)}, bf16[8192,128]{1,0:T(8,128)(2,1)}, u32[]{:S(2)}) copy-start(bf16[8192,128]{1,0:T(8,128)(2,1)} %param.14) | copy-start | bytes 6291460
  6.5 59.6 %copy-start.5 = (f32[8192]{0:T(1024)S(1)}, f32[8192]{0:T(1024)}, u32[]{:S(2)}) copy-start(f32[8192]{0:T(1024)} %param.12) | copy-start | bytes 98308
  6.5 56.3 %all-gather.2.cloned.1.call-start = ((), (), s32[]{:S(2)}) async-start(), calls=%async_computation.3 | async-start | bytes 4456448 | tf_op jit(solution)/shard_map/all_gather | solution.py:24
  62.9 3.4 %copy-start.2 = (bf16[256,8192]{1,0:T(8,128)(2,1)S(1)}, bf16[256,8192]{1,0:T(8,128)(2,1)}, u32[]{:S(2)}) copy-start(bf16[256,8192]{1,0:T(8,128)(2,1)} %all-gather.2.cloned.1.call-done) | copy-start | bytes 12582916
  72.2 1.5 copy-start.3
  72.2 7.6 %copy-start.4 = (s32[256]{0:T(256)S(1)}, s32[256]{0:T(256)}, u32[]{:S(2)}) copy-start(s32[256]{0:T(256)} %param.18) | copy-start | bytes 3076
  76.1 15.2 %all-to-all-start = ((bf16[16,2,5120]{2,1,0:T(2,128)(2,1)}), bf16[16,2,5120]{2,1,0:T(2,128)(2,1)S(1)}, u32[]{:S(2)}, u32[]{:S(2)}) async-start(bf16[16,2,5120]{2,1,0:T(2,128)(2,1)} %reshape.91), calls=%async_computation | async-start | bytes 655360 | tf_op jit(solution)/shard_map/all_to_all | solution.py:36
  79.7 163.7 %reduce-scatter.2.cloned.1.call-start = ((), (), s32[]{:S(2)}) async-start(), calls=%async_computation.4 | async-start | bytes 4456448 | tf_op jit(solution)/shard_map/reduce_scatter | solution.py:107
  165.1 78.3 %copy-start.1 = (bf16[8192,128]{1,0:T(8,128)(2,1)S(1)}, bf16[8192,128]{1,0:T(8,128)(2,1)}, u32[]{:S(2)}) copy-start(bf16[8192,128]{1,0:T(8,128)(2,1)} %param.14) | copy-start | bytes 6291460
Sparse Core Ops, SparseCore 0:
  9.6 53.2 all-gather.1
  173.2 70.1 reduce-scatter.1
where the time goes:
time: 251 us; the launch traced here: 250 us
  waiting for transfers between devices  138 us (55%)
  local copies, waits for them, and re-layouts  44.6 us (18%)
  matrix products  31.8 us (13%)
  between operations  13.6 us (5%)
  blocking collectives  12.9 us (5%)
  other arithmetic  5.55 us (2%)
  starting transfers between devices  3.58 us (1%)
    reduce_scatter x1, waiting for transfers between devices, body(): lax.psum_scatter(jnp.dot(in_requests, w_out, preferred_element_type=jnp.f...  70.3 us
    all_gather x1, waiting for transfers between devices, body(): lax.all_gather(rows, ('pool', 'tensor'), axis=0, tiled=True)  55.6 us
    dynamic_slice x4, local copies, waits for them, and re-layouts, visit(): lax.dynamic_slice_in_dim(value_cache, begin, block, 1)  29.4 us
    all_to_all x1, blocking collectives, body(): lax.all_to_all(attended.reshape(slots_dev, devices, piece_cols), ('pool',...  12.9 us
    dynamic_slice x2, local copies, waits for them, and re-layouts, visit(): lax.dynamic_slice_in_dim(key_cache, begin, block, 1)  12.7 us
    all_to_all x1, waiting for transfers between devices, body(): lax.all_to_all(in_slots.reshape(requests, 1, width), ('pool', 'tensor'),...  11.4 us
    dot_general x2, matrix products, visit(): jnp.einsum('skgl,slkd->skgd', probs.astype(jnp.bfloat16), values_blk, pre...  8.98 us
    dot_general x1, matrix products, body(): jnp.dot(in_requests, w_out, preferred_element_type=jnp.float32)  7.98 us
  transfers between devices with their start and end apart: 3, of which 3 were waited for; matrix products, arithmetic and copies ran while one was open for 0% of the time, Pallas kernels for 0%

commit v1 on v0

v1 whole, which is shorter than its diff:
```python
import functools

import jax
import jax.numpy as jnp
from jax import lax
from jax.experimental import pallas as pl
from jax.experimental.pallas import tpu as pltpu
from jax.sharding import PartitionSpec as P

HD = 128
EPS = 1e-05
HALVES = 2
SUBS = 4
MESH = pl.DeviceIdType.MESH


def kernel(
    cfg,
    lens_ref, rows_ref, gain_ref, sort_ref, back_ref, wq_hbm, wkv_hbm, wo_hbm, k_hbm, v_hbm,
    out_ref,
    x_buf, wq, wkv, wo, kc, vc, acc_q, acc_kv, cols, sendq, arrived, qbuf, kbuf, vbuf, kvflat,
    obuf, sendo, returned, inr, pbuf, recvp, first, rbuf,
    load_sem, ag_send, ag_recv, core_send, core_recv, a_send, a_recv, b_send, b_recv,
    p_send, p_recv, r_send, r_recv,
):
    pools, ring, heads, kvh, rows_dev = cfg
    n = pools * ring
    group = heads // kvh
    slots_dev, length = kc.shape[0], kc.shape[1]
    depth = rows_ref.shape[1]
    query_cols = wq.shape[1]
    kv_cols = wkv.shape[1]
    scale = HD ** (-0.5)
    pool = lax.axis_index("pool")
    t_me = lax.axis_index("tensor")
    me = pool * ring + t_me
    half_ring = ring // 2

    def tensor_at(p):
        high = p // half_ring
        return (1 - high) * (2 * p) + high * (2 * (ring - 1 - p) + 1)

    odd = lax.rem(t_me, 2)
    pos = (1 - odd) * (t_me // 2) + odd * (ring - 1 - t_me // 2)

    def at(offset):
        return tensor_at(lax.rem(pos + offset + 2 * ring, ring))

    right = {"tensor": at(1)}
    left = {"tensor": at(-1)}
    other = {"pool": 1 - pool}

    loads = [
        pltpu.make_async_copy(src, dst, load_sem.at[i])
        for i, (src, dst) in enumerate(
            [(wq_hbm, wq), (wkv_hbm, wkv), (k_hbm, kc), (v_hbm, vc), (wo_hbm, wo)]
        )
    ]
    barrier = pltpu.get_barrier_semaphore()

    def greet(o, _):
        peer = lax.rem(me + o, n)
        pl.semaphore_signal(
            barrier, inc=1, device_id={"pool": peer // ring, "tensor": lax.rem(peer, ring)},
            device_id_type=MESH,
        )
        return 0

    lax.fori_loop(1, n, greet, 0)
    for load in loads:
        load.start()

    def rows_of(p, t):
        return pl.ds(pl.multiple_of((p * ring + t) * rows_dev, rows_dev), rows_dev)

    values = rows_ref[...].astype(jnp.float32)
    normed = values * lax.rsqrt(jnp.mean(values * values, axis=1, keepdims=True) + EPS)
    x_buf[rows_of(pool, t_me), :] = (normed * gain_ref[...]).astype(jnp.bfloat16)
    pl.semaphore_wait(barrier, n - 1)

    width = depth // HALVES

    def block(p, t, c):
        return x_buf.at[rows_of(p, t), pl.ds(c * width, width)]

    sent = []

    def ring_copy(way, dist, c):
        t = at(-dist) if way == 0 else at(dist)
        ref = block(pool, t, c)
        return pltpu.make_async_remote_copy(
            ref, ref, ag_send.at[way, dist - 1, c], ag_recv.at[way, dist - 1, c],
            device_id=right if way == 0 else left, device_id_type=MESH,
        )

    def ring_send(way, dist, c):
        t = at(-(dist - 1)) if way == 0 else at(dist - 1)
        ref = block(pool, t, c)
        copy = pltpu.make_async_remote_copy(
            ref, ref, ag_send.at[way, dist - 1, c], ag_recv.at[way, dist - 1, c],
            device_id=right if way == 0 else left, device_id_type=MESH,
        )
        copy.start()
        sent.append(copy)

    def core_copy(p, k, c):
        ref = block(p, at(k), c)
        return pltpu.make_async_remote_copy(
            ref, ref, core_send.at[k, c], core_recv.at[k, c], device_id=other, device_id_type=MESH,
        )

    def core_send_start(k, c):
        copy = core_copy(pool, k % ring, c)
        copy.start()
        sent.append(copy)

    def travels(way, dist, c):
        return dist < half_ring or (dist == half_ring and c == way)

    for c in range(HALVES):
        for way in range(2):
            cc = c if way == 0 else HALVES - 1 - c
            if travels(way, 1, cc):
                ring_send(way, 1, cc)
    for c in range(HALVES):
        core_send_start(0, c)
    for dist in range(1, half_ring + 1):
        for c in range(HALVES):
            for way in range(2):
                cc = c if way == 0 else HALVES - 1 - c
                if travels(way, dist, cc):
                    ring_copy(way, dist, cc).wait_recv()
                    if travels(way, dist + 1, cc):
                        ring_send(way, dist + 1, cc)
                    core_send_start(-dist if way == 0 else dist, cc)
    for k in range(ring):
        for c in range(HALVES):
            core_copy(1 - pool, k, c).wait_recv()
    for copy in sent:
        copy.wait_send()

    loads[0].wait()
    loads[1].wait()

    acc_q[...] = jnp.zeros_like(acc_q)
    acc_kv[...] = jnp.zeros_like(acc_kv)
    step = depth // 8

    def project(i, _):
        ks = pl.ds(pl.multiple_of(i * step, step), step)
        acc_q[...] += jnp.dot(x_buf[:, ks], wq[ks, :], preferred_element_type=jnp.float32)
        acc_kv[...] += jnp.dot(x_buf[:, ks], wkv[ks, :], preferred_element_type=jnp.float32)
        return 0

    lax.fori_loop(0, 8, project, 0)
    cols[:, :query_cols] = acc_q[...].astype(jnp.bfloat16)
    cols[:, query_cols:] = acc_kv[...].astype(jnp.bfloat16)
    in_slots = jnp.dot(sort_ref[...], cols[...], preferred_element_type=jnp.float32).astype(jnp.bfloat16)
    sendq[...] = in_slots.reshape(sendq.shape)

    def exchange(src, dst, s_sem, r_sem):
        def copy_to(peer, slot):
            return pltpu.make_async_remote_copy(
                src.at[peer], dst.at[slot], s_sem.at[peer], r_sem.at[slot],
                device_id={"pool": peer // ring, "tensor": lax.rem(peer, ring)},
                device_id_type=MESH,
            )

        def start(o, _):
            copy_to(lax.rem(me + o, n), me).start()
            return 0

        def finish(o, _):
            peer = lax.rem(me + o, n)
            copy_to(peer, peer).wait()
            return 0

        lax.fori_loop(1, n, start, 0)
        dst[me] = src[me]
        lax.fori_loop(1, n, finish, 0)

    exchange(sendq, arrived, a_send, a_recv)

    hp = query_cols // HD
    for i in range(n):
        for j in range(hp):
            qbuf[:, i * hp + j, :] = arrived[i, :, j * HD:(j + 1) * HD].astype(jnp.float32)
        kvflat[:, i * kv_cols:(i + 1) * kv_cols] = arrived[i, :, query_cols:].astype(jnp.float32)
    for k in range(kvh):
        kbuf[:, k, :] = kvflat[:, k * HD:(k + 1) * HD]
        vbuf[:, k, :] = kvflat[:, (kvh + k) * HD:(kvh + k + 1) * HD]
    loads[2].wait()
    loads[3].wait()

    row_head = lax.broadcasted_iota(jnp.int32, (heads, kvh * HD), 0) // group
    col_head = lax.broadcasted_iota(jnp.int32, (heads, kvh * HD), 1) // HD
    diagonal = row_head == col_head

    def attend(s):
        q = qbuf[s]
        wide = jnp.where(diagonal, jnp.concatenate([q] * kvh, axis=1), 0.0).astype(jnp.bfloat16)
        scores = lax.dot_general(
            wide, kc[s], (((1,), (1,)), ((), ())), preferred_element_type=jnp.float32
        ) * scale
        live = lax.broadcasted_iota(jnp.int32, (heads, length), 1) < lens_ref[s]
        scores = jnp.where(live, scores, -1e30)
        nk = jnp.broadcast_to(kbuf[s][:, None, :], (kvh, group, HD)).reshape(heads, HD)
        nv = jnp.broadcast_to(vbuf[s][:, None, :], (kvh, group, HD)).reshape(heads, HD)
        own = jnp.sum(q * nk, axis=1, keepdims=True) * scale
        top = jnp.maximum(jnp.max(scores, axis=1, keepdims=True), own)
        probs = jnp.exp(scores - top)
        own_prob = jnp.exp(own - top)
        totals = jnp.sum(probs, axis=1, keepdims=True) + own_prob
        full = jnp.dot(probs.astype(jnp.bfloat16), vc[s], preferred_element_type=jnp.float32)
        mine = jnp.concatenate(
            [full[k * group:(k + 1) * group, k * HD:(k + 1) * HD] for k in range(kvh)], axis=0
        )
        mine = mine + own_prob.astype(jnp.bfloat16).astype(jnp.float32) * nv
        obuf[s] = mine / totals

    def attend_pair(i, _):
        attend(2 * i)
        attend(2 * i + 1)
        return 0

    lax.fori_loop(0, slots_dev // 2, attend_pair, 0)

    for i in range(n):
        for j in range(hp):
            sendo[i, :, j * HD:(j + 1) * HD] = obuf[:, i * hp + j, :].astype(jnp.bfloat16)
    exchange(sendo, returned, b_send, b_recv)

    requests = n * rows_dev
    inr[...] = jnp.dot(
        back_ref[...], returned[...].reshape(requests, query_cols), preferred_element_type=jnp.float32
    ).astype(jnp.bfloat16)
    loads[4].wait()

    tiles = 2 * SUBS
    tile = depth // tiles
    half_rows = ring * rows_dev

    def pair_copy(c):
        return pltpu.make_async_remote_copy(
            pbuf.at[c, pl.ds(pl.multiple_of((1 - pool) * half_rows, half_rows), half_rows)],
            recvp.at[c], p_send.at[c], p_recv.at[c], device_id=other, device_id_type=MESH,
        )

    for sub in range(SUBS):
        for way in range(2):
            c = way * SUBS + sub
            pbuf[c] = jnp.dot(
                inr[...], wo[:, c * tile:(c + 1) * tile], preferred_element_type=jnp.float32
            ).astype(jnp.bfloat16)
            pair_copy(c).start()

    def pair_sum(c, t):
        mine = pbuf[c, rows_of(pool, t), :].astype(jnp.float32)
        theirs = recvp[c, pl.ds(pl.multiple_of(t * rows_dev, rows_dev), rows_dev), :]
        return mine + theirs.astype(jnp.float32)

    def hop_copy(src, way, hop, sub):
        return pltpu.make_async_remote_copy(
            src, rbuf.at[way, hop, sub], r_send.at[way, hop, sub], r_recv.at[way, hop, sub],
            device_id=right if way == 0 else left, device_id_type=MESH,
        )

    for sub in range(SUBS):
        for way in range(2):
            c = way * SUBS + sub
            pair_copy(c).wait_recv()
            t = at(-1) if way == 0 else at(1)
            first[way, sub] = pair_sum(c, t).astype(jnp.bfloat16)
            hop_copy(first.at[way, sub], way, 0, sub).start()

    def hop_step(hop, _):
        for sub in range(SUBS):
            for way in range(2):
                c = way * SUBS + sub
                here = rbuf.at[way, hop, sub]
                hop_copy(here, way, hop, sub).wait_recv()
                t = at(-2 - hop) if way == 0 else at(2 + hop)
                rbuf[way, hop, sub] = (
                    rbuf[way, hop, sub].astype(jnp.float32) + pair_sum(c, t)
                ).astype(jnp.bfloat16)
                hop_copy(here, way, hop + 1, sub).start()
        return 0

    lax.fori_loop(0, ring - 2, hop_step, 0)
    last = ring - 2
    for sub in range(SUBS):
        for way in range(2):
            c = way * SUBS + sub
            hop_copy(rbuf.at[way, last, sub], way, last, sub).wait_recv()
            out_ref[:, c * tile:(c + 1) * tile] = (
                rbuf[way, last, sub].astype(jnp.float32) + pair_sum(c, t_me)
            ).astype(out_ref.dtype)

    for sub in range(SUBS):
        for way in range(2):
            pair_copy(way * SUBS + sub).wait_send()
            hop_copy(first.at[way, sub], way, 0, sub).wait_send()

    def drain(hop, _):
        for sub in range(SUBS):
            for way in range(2):
                hop_copy(rbuf.at[way, hop - 1, sub], way, hop, sub).wait_send()
        return 0

    lax.fori_loop(1, ring - 1, drain, 0)


def body(rows, norm_gain, w_query, w_keyval, w_out, key_cache, value_cache, lengths, slot_of):
    pools, ring = lax.axis_size("pool"), lax.axis_size("tensor")
    n = pools * ring
    rows_dev, depth = rows.shape
    slots_dev, length, kv_width = key_cache.shape
    kvh = kv_width // HD
    query_cols, kv_cols = w_query.shape[1], w_keyval.shape[1]
    heads = query_cols * n // HD
    width = query_cols + kv_cols
    requests = rows_dev * n
    half_ring = ring // 2
    tile = depth // (2 * SUBS)
    slot_ids = jnp.arange(requests, dtype=jnp.int32)
    sort_map = (slot_of[None, :] == slot_ids[:, None]).astype(jnp.bfloat16)
    back_map = (slot_of[:, None] == slot_ids[None, :]).astype(jnp.bfloat16)
    own_slots = lax.axis_index(("pool", "tensor")) * slots_dev + jnp.arange(slots_dev, dtype=jnp.int32)
    slot_len = jnp.sum(jnp.where(slot_of[None, :] == own_slots[:, None], lengths[None, :], 0), axis=1)
    bf16, f32 = jnp.bfloat16, jnp.float32
    vmem = pl.BlockSpec(memory_space=pltpu.VMEM)
    hbm = pl.BlockSpec(memory_space=pl.ANY)
    dma = pltpu.SemaphoreType.DMA
    return pl.pallas_call(
        functools.partial(kernel, (pools, ring, heads, kvh, rows_dev)),
        out_shape=jax.ShapeDtypeStruct((rows_dev, depth), bf16),
        in_specs=[pl.BlockSpec(memory_space=pltpu.SMEM)] + [vmem] * 4 + [hbm] * 5,
        out_specs=vmem,
        scratch_shapes=[
            pltpu.VMEM((requests, depth), bf16),
            pltpu.VMEM(w_query.shape, bf16),
            pltpu.VMEM(w_keyval.shape, bf16),
            pltpu.VMEM(w_out.shape, bf16),
            pltpu.VMEM(key_cache.shape, bf16),
            pltpu.VMEM(value_cache.shape, bf16),
            pltpu.VMEM((requests, query_cols), f32),
            pltpu.VMEM((requests, kv_cols), f32),
            pltpu.VMEM((requests, width), bf16),
            pltpu.VMEM((n, slots_dev, width), bf16),
            pltpu.VMEM((n, slots_dev, width), bf16),
            pltpu.VMEM((slots_dev, heads, HD), f32),
            pltpu.VMEM((slots_dev, kvh, HD), f32),
            pltpu.VMEM((slots_dev, kvh, HD), f32),
            pltpu.VMEM((slots_dev, 2 * kvh * HD), f32),
            pltpu.VMEM((slots_dev, heads, HD), f32),
            pltpu.VMEM((n, slots_dev, query_cols), bf16),
            pltpu.VMEM((n, slots_dev, query_cols), bf16),
            pltpu.VMEM((requests, query_cols), bf16),
            pltpu.VMEM((2 * SUBS, requests, tile), bf16),
            pltpu.VMEM((2 * SUBS, requests // pools, tile), bf16),
            pltpu.VMEM((2, SUBS, rows_dev, tile), bf16),
            pltpu.VMEM((2, ring - 1, SUBS, rows_dev, tile), bf16),
            dma((5,)),
            dma((2, half_ring, HALVES)),
            dma((2, half_ring, HALVES)),
            dma((ring, HALVES)),
            dma((ring, HALVES)),
            dma((n,)),
            dma((n,)),
            dma((n,)),
            dma((n,)),
            dma((2 * SUBS,)),
            dma((2 * SUBS,)),
            dma((2, ring - 1, SUBS)),
            dma((2, ring - 1, SUBS)),
        ],
        compiler_params=pltpu.CompilerParams(
            collective_id=0, has_side_effects=True, vmem_limit_bytes=60 * 2**20
        ),
        name="decode_step",
    )(
        slot_len, rows, norm_gain.reshape(1, depth), sort_map, back_map,
        w_query, w_keyval, w_out, key_cache, value_cache,
    )


def solution(mesh):
    placed = (
        P(("groups", "pool", "tensor"), None),
        P(),
        P(None, ("pool", "tensor")),
        P(None, ("pool", "tensor")),
        P(("pool", "tensor"), None),
        P(("groups", "pool", "tensor"), None, None),
        P(("groups", "pool", "tensor"), None, None),
        P("groups"),
        P("groups"),
    )
    return jax.shard_map(
        body,
        mesh=mesh,
        in_specs=placed,
        out_specs=P(("groups", "pool", "tensor"), None),
        check_vma=False,
    )
```

time: 251 us -> 99.6 us (0.40)
  waiting for transfers between devices: 138 us -> 0 us
  Pallas kernels: 0 us -> 94.7 us
  local copies, waits for them, and re-layouts: 44.6 us -> 1.67 us
  matrix products: 31.8 us -> 0 us
  between operations: 13.6 us -> 0.01 us
  blocking collectives: 12.9 us -> 0 us
  starting transfers between devices: 3.58 us -> 0 us
  other arithmetic: 5.55 us -> 2.97 us
    pallas_call x0 -> x1, Pallas kernels: none -> 94.7 us  [body(): pl.pallas_call(functools.partial(kernel, (pools, ring, heads, kvh, rows_d...]
    reduce_scatter x1 -> x0, waiting for transfers between devices: 70.3 us -> none  [body(): lax.psum_scatter(jnp.dot(in_requests, w_out, preferred_element_type=jnp.f...]
    all_gather x1 -> x0, waiting for transfers between devices: 55.6 us -> none  [body(): lax.all_gather(rows, ('pool', 'tensor'), axis=0, tiled=True)]
    dynamic_slice x6 -> x0, local copies, waits for them, and re-layouts: 42.1 us -> none  [the longest x4 29.4 us: visit(): lax.dynamic_slice_in_dim(value_cache, begin, block, 1)]
    dot_general x9 -> x0, matrix products: 31.8 us -> none  [the longest x2 8.98 us: visit(): jnp.einsum('skgl,slkd->skgd', probs.astype(jnp.bfloat16), values_blk, pre...]
    all_to_all x1 -> x0, blocking collectives: 12.9 us -> none  [body(): lax.all_to_all(attended.reshape(slots_dev, devices, piece_cols), ('pool',...]
    all_to_all x1 -> x0, waiting for transfers between devices: 11.4 us -> none  [body(): lax.all_to_all(in_slots.reshape(requests, 1, width), ('pool', 'tensor'),...]
    reduce_sum x3 -> x0, other arithmetic: 4.05 us -> none  [the longest x1 3.25 us: body(): jnp.mean(values32 * values32, axis=1, keepdims=True) + EPS]
  transfers between devices with their start and end apart: 3 -> 0, of which waited for: 3 -> 0; matrix products, arithmetic and copies ran while one was open for 0% -> 0% of each run, Pallas kernels for 0% -> 0%
where the time goes in v1:
time: 99.6 us; the launch traced here: 99.4 us
  Pallas kernels  94.7 us (95%)
  other arithmetic  2.97 us (3%)
  local copies, waits for them, and re-layouts  1.67 us (2%)
    pallas_call x1, Pallas kernels, body(): pl.pallas_call(functools.partial(kernel, (pools, ring, heads, kvh, rows_d...  94.7 us

profile of v1, /device:TPU:0, one launch (start us, length us, event | category | flops | bytes accessed | tf_op | source)
XLA Modules:
  0.0 99.4 jit_solution(2998858846636570905)
XLA Ops:
  0.0 1.5 %select_reduce_fusion.lens_ref = s32[16]{0:T(128)} fusion(s32[256]{0:T(256)} %param.16, s32[256]{0:T(256)} %param.17, s32[16]{0:T(128)S(1)} %iota_add_fusion), kind=kLoop, calls=%fused_computation.4 | loop fusion | flops 12272 | bytes 2176 | tf_op jit(solution)/shard_map/reduce_sum | solution.py:329
  1.5 1.5 %fusion.1 = (bf16[256,256]{1,0:T(8,128)(2,1)}, bf16[256,256]{1,0:T(8,128)(2,1)}) fusion(s32[256]{0:T(256)} %param.17), kind=kLoop, calls=%fused_computation.3 | loop fusion | flops 262144 | bytes 263168 | tf_op jit(solution)/shard_map/convert_element_type | solution.py:327
  3.0 94.7 %decode_step.1 = bf16[16,8192]{1,0:T(8,128)(2,1)} custom-call(s32[16]{0:T(128)} %select_reduce_fusion.lens_ref, bf16[16,8192]{1,0:T(8,128)(2,1)} %rows_ref.1, f32[1,8192]{1,0:T(1,128)} %bitcast.1, bf16[256,256]{1,0:T(8,128)(2,1)} %get-tuple-element.6.sort_ref, bf16[256,256]{1,0:T(8,128)(2,1)} %get-tuple-element.5.back_ref, bf16[8192,512]{1,0:T(8,128)(2,1)} %wq_hbm.1, ...), custom_call_target="tpu_custom_call" | custom-call | tf_op jit(solution)/shard_map/decode_step/pallas_call | solution.py:334
  97.7 1.7 %copy.11 = bf16[16,8192]{1,0:T(8,128)(2,1)} copy(bf16[16,8192]{1,0:T(8,128)(2,1)} %decode_step.1) | data formatting | bytes 524288
  (1 shorter events, 0.0 us)

commit v2 on v1

--- a/solution.py
+++ b/solution.py
@@ -9,17 +9,18 @@
 
 HD = 128
 EPS = 1e-05
-HALVES = 2
+CHUNKS = 4
 SUBS = 4
+TOGETHER = 4
 MESH = pl.DeviceIdType.MESH
 
 
 def kernel(
     cfg,
-    lens_ref, rows_ref, gain_ref, sort_ref, back_ref, wq_hbm, wkv_hbm, wo_hbm, k_hbm, v_hbm,
+    slots_ref, lens_ref, rows_ref, gain_ref, wq_hbm, wkv_hbm, wo_hbm, k_hbm, v_hbm,
     out_ref,
     x_buf, wq, wkv, wo, kc, vc, acc_q, acc_kv, cols, sendq, arrived, qbuf, kbuf, vbuf, kvflat,
-    obuf, sendo, returned, inr, pbuf, recvp, first, rbuf,
+    obuf, sendo, returned, sort_map, lens, inr, pbuf, recvp, first, rbuf,
     load_sem, ag_send, ag_recv, core_send, core_recv, a_send, a_recv, b_send, b_recv,
     p_send, p_recv, r_send, r_recv,
 ):
@@ -67,8 +68,6 @@
         return 0
 
     lax.fori_loop(1, n, greet, 0)
-    for load in loads:
-        load.start()
 
     def rows_of(p, t):
         return pl.ds(pl.multiple_of((p * ring + t) * rows_dev, rows_dev), rows_dev)
@@ -78,7 +77,7 @@
     x_buf[rows_of(pool, t_me), :] = (normed * gain_ref[...]).astype(jnp.bfloat16)
     pl.semaphore_wait(barrier, n - 1)
 
-    width = depth // HALVES
+    width = depth // CHUNKS
 
     def block(p, t, c):
         return x_buf.at[rows_of(p, t), pl.ds(c * width, width)]
@@ -115,29 +114,43 @@
         sent.append(copy)
 
     def travels(way, dist, c):
-        return dist < half_ring or (dist == half_ring and c == way)
-
-    for c in range(HALVES):
+        return dist < half_ring or (dist == half_ring and c * 2 // CHUNKS == way)
+
+    for c in range(CHUNKS):
         for way in range(2):
-            cc = c if way == 0 else HALVES - 1 - c
+            cc = c if way == 0 else CHUNKS - 1 - c
             if travels(way, 1, cc):
                 ring_send(way, 1, cc)
-    for c in range(HALVES):
+    for c in range(CHUNKS):
         core_send_start(0, c)
+    loads[0].start()
+    loads[1].start()
+
+    requests = n * rows_dev
+    slot_row = slots_ref[...]
+    sort_map[...] = jnp.where(
+        lax.broadcasted_iota(jnp.int32, (requests, requests), 0) == slot_row, 1.0, 0.0
+    ).astype(jnp.bfloat16)
+    own_slots = lax.broadcasted_iota(jnp.int32, (slots_dev, requests), 0) + me * slots_dev
+    own_len = jnp.sum(
+        jnp.where(own_slots == slot_row, lens_ref[...].astype(jnp.float32), 0.0), axis=1, keepdims=True
+    )
+    lens[...] = jnp.broadcast_to(own_len, lens.shape)
+
     for dist in range(1, half_ring + 1):
-        for c in range(HALVES):
+        for c in range(CHUNKS):
             for way in range(2):
-                cc = c if way == 0 else HALVES - 1 - c
+                cc = c if way == 0 else CHUNKS - 1 - c
                 if travels(way, dist, cc):
                     ring_copy(way, dist, cc).wait_recv()
                     if travels(way, dist + 1, cc):
                         ring_send(way, dist + 1, cc)
                     core_send_start(-dist if way == 0 else dist, cc)
+        if dist <= 2:
+            loads[1 + dist].start()
     for k in range(ring):
-        for c in range(HALVES):
+        for c in range(CHUNKS):
             core_copy(1 - pool, k, c).wait_recv()
-    for copy in sent:
-        copy.wait_send()
 
     loads[0].wait()
     loads[1].wait()
@@ -155,7 +168,7 @@
     lax.fori_loop(0, 8, project, 0)
     cols[:, :query_cols] = acc_q[...].astype(jnp.bfloat16)
     cols[:, query_cols:] = acc_kv[...].astype(jnp.bfloat16)
-    in_slots = jnp.dot(sort_ref[...], cols[...], preferred_element_type=jnp.float32).astype(jnp.bfloat16)
+    in_slots = jnp.dot(sort_map[...], cols[...], preferred_element_type=jnp.float32).astype(jnp.bfloat16)
     sendq[...] = in_slots.reshape(sendq.shape)
 
     def exchange(src, dst, s_sem, r_sem):
@@ -179,6 +192,7 @@
         dst[me] = src[me]
         lax.fori_loop(1, n, finish, 0)
 
+    loads[4].start()
     exchange(sendq, arrived, a_send, a_recv)
 
     hp = query_cols // HD
@@ -193,6 +207,7 @@
     loads[3].wait()
 
     row_head = lax.broadcasted_iota(jnp.int32, (heads, kvh * HD), 0) // group
+    place = lax.broadcasted_iota(jnp.int32, (heads, length), 1).astype(jnp.float32)
     col_head = lax.broadcasted_iota(jnp.int32, (heads, kvh * HD), 1) // HD
     diagonal = row_head == col_head
 
@@ -202,8 +217,7 @@
         scores = lax.dot_general(
             wide, kc[s], (((1,), (1,)), ((), ())), preferred_element_type=jnp.float32
         ) * scale
-        live = lax.broadcasted_iota(jnp.int32, (heads, length), 1) < lens_ref[s]
-        scores = jnp.where(live, scores, -1e30)
+        scores = jnp.where(place < lens[pl.ds(s, 1), :], scores, -1e30)
         nk = jnp.broadcast_to(kbuf[s][:, None, :], (kvh, group, HD)).reshape(heads, HD)
         nv = jnp.broadcast_to(vbuf[s][:, None, :], (kvh, group, HD)).reshape(heads, HD)
         own = jnp.sum(q * nk, axis=1, keepdims=True) * scale
@@ -218,21 +232,21 @@
         mine = mine + own_prob.astype(jnp.bfloat16).astype(jnp.float32) * nv
         obuf[s] = mine / totals
 
-    def attend_pair(i, _):
-        attend(2 * i)
-        attend(2 * i + 1)
+    def attend_some(i, _):
+        for j in range(TOGETHER):
+            attend(TOGETHER * i + j)
         return 0
 
-    lax.fori_loop(0, slots_dev // 2, attend_pair, 0)
+    lax.fori_loop(0, slots_dev // TOGETHER, attend_some, 0)
 
     for i in range(n):
         for j in range(hp):
             sendo[i, :, j * HD:(j + 1) * HD] = obuf[:, i * hp + j, :].astype(jnp.bfloat16)
     exchange(sendo, returned, b_send, b_recv)
 
-    requests = n * rows_dev
-    inr[...] = jnp.dot(
-        back_ref[...], returned[...].reshape(requests, query_cols), preferred_element_type=jnp.float32
+    inr[...] = lax.dot_general(
+        sort_map[...], returned[...].reshape(requests, query_cols), (((0,), (0,)), ((), ())),
+        preferred_element_type=jnp.float32,
     ).astype(jnp.bfloat16)
     loads[4].wait()
 
@@ -245,6 +259,25 @@
             pbuf.at[c, pl.ds(pl.multiple_of((1 - pool) * half_rows, half_rows), half_rows)],
             recvp.at[c], p_send.at[c], p_recv.at[c], device_id=other, device_id_type=MESH,
         )
+
+    def pair_sum(c, t):
+        mine = pbuf[c, rows_of(pool, t), :].astype(jnp.float32)
+        theirs = recvp[c, pl.ds(pl.multiple_of(t * rows_dev, rows_dev), rows_dev), :]
+        return mine + theirs.astype(jnp.float32)
+
+    def hop_copy(src, way, hop, sub):
+        return pltpu.make_async_remote_copy(
+            src, rbuf.at[way, hop, sub], r_send.at[way, hop, sub], r_recv.at[way, hop, sub],
+            device_id=right if way == 0 else left, device_id_type=MESH,
+        )
+
+    def set_off(sub):
+        for way in range(2):
+            c = way * SUBS + sub
+            pair_copy(c).wait_recv()
+            t = at(-1) if way == 0 else at(1)
+            first[way, sub] = pair_sum(c, t).astype(jnp.bfloat16)
+            hop_copy(first.at[way, sub], way, 0, sub).start()
 
     for sub in range(SUBS):
         for way in range(2):
@@ -253,25 +286,9 @@
                 inr[...], wo[:, c * tile:(c + 1) * tile], preferred_element_type=jnp.float32
             ).astype(jnp.bfloat16)
             pair_copy(c).start()
-
-    def pair_sum(c, t):
-        mine = pbuf[c, rows_of(pool, t), :].astype(jnp.float32)
-        theirs = recvp[c, pl.ds(pl.multiple_of(t * rows_dev, rows_dev), rows_dev), :]
-        return mine + theirs.astype(jnp.float32)
-
-    def hop_copy(src, way, hop, sub):
-        return pltpu.make_async_remote_copy(
-            src, rbuf.at[way, hop, sub], r_send.at[way, hop, sub], r_recv.at[way, hop, sub],
-            device_id=right if way == 0 else left, device_id_type=MESH,
-        )
-
-    for sub in range(SUBS):
-        for way in range(2):
-            c = way * SUBS + sub
-            pair_copy(c).wait_recv()
-            t = at(-1) if way == 0 else at(1)
-            first[way, sub] = pair_sum(c, t).astype(jnp.bfloat16)
-            hop_copy(first.at[way, sub], way, 0, sub).start()
+        if sub >= 1:
+            set_off(sub - 1)
+    set_off(SUBS - 1)
 
     def hop_step(hop, _):
         for sub in range(SUBS):
@@ -308,6 +325,8 @@
         return 0
 
     lax.fori_loop(1, ring - 1, drain, 0)
+    for copy in sent:
+        copy.wait_send()
 
 
 def body(rows, norm_gain, w_query, w_keyval, w_out, key_cache, value_cache, lengths, slot_of):
@@ -322,11 +341,6 @@
     requests = rows_dev * n
     half_ring = ring // 2
     tile = depth // (2 * SUBS)
-    slot_ids = jnp.arange(requests, dtype=jnp.int32)
-    sort_map = (slot_of[None, :] == slot_ids[:, None]).astype(jnp.bfloat16)
-    back_map = (slot_of[:, None] == slot_ids[None, :]).astype(jnp.bfloat16)
-    own_slots = lax.axis_index(("pool", "tensor")) * slots_dev + jnp.arange(slots_dev, dtype=jnp.int32)
-    slot_len = jnp.sum(jnp.where(slot_of[None, :] == own_slots[:, None], lengths[None, :], 0), axis=1)
     bf16, f32 = jnp.bfloat16, jnp.float32
     vmem = pl.BlockSpec(memory_space=pltpu.VMEM)
     hbm = pl.BlockSpec(memory_space=pl.ANY)
@@ -334,7 +348,7 @@
     return pl.pallas_call(
         functools.partial(kernel, (pools, ring, heads, kvh, rows_dev)),
         out_shape=jax.ShapeDtypeStruct((rows_dev, depth), bf16),
-        in_specs=[pl.BlockSpec(memory_space=pltpu.SMEM)] + [vmem] * 4 + [hbm] * 5,
+        in_specs=[vmem] * 4 + [hbm] * 5,
         out_specs=vmem,
         scratch_shapes=[
             pltpu.VMEM((requests, depth), bf16),
@@ -355,16 +369,18 @@
             pltpu.VMEM((slots_dev, heads, HD), f32),
             pltpu.VMEM((n, slots_dev, query_cols), bf16),
             pltpu.VMEM((n, slots_dev, query_cols), bf16),
+            pltpu.VMEM((requests, requests), bf16),
+            pltpu.VMEM((slots_dev, length), f32),
             pltpu.VMEM((requests, query_cols), bf16),
             pltpu.VMEM((2 * SUBS, requests, tile), bf16),
             pltpu.VMEM((2 * SUBS, requests // pools, tile), bf16),
             pltpu.VMEM((2, SUBS, rows_dev, tile), bf16),
             pltpu.VMEM((2, ring - 1, SUBS, rows_dev, tile), bf16),
             dma((5,)),
-            dma((2, half_ring, HALVES)),
-            dma((2, half_ring, HALVES)),
-            dma((ring, HALVES)),
-            dma((ring, HALVES)),
+            dma((2, half_ring, CHUNKS)),
+            dma((2, half_ring, CHUNKS)),
+            dma((ring, CHUNKS)),
+            dma((ring, CHUNKS)),
             dma((n,)),
             dma((n,)),
             dma((n,)),
@@ -379,7 +395,7 @@
         ),
         name="decode_step",
     )(
-        slot_len, rows, norm_gain.reshape(1, depth), sort_map, back_map,
+        slot_of.reshape(1, requests), lengths.reshape(1, requests), rows, norm_gain.reshape(1, depth),
         w_query, w_keyval, w_out, key_cache, value_cache,
     )
 

time: 99.6 us -> 95.3 us (0.957)
  other arithmetic: 2.97 us -> 0 us
  Pallas kernels: 94.7 us -> 93.5 us
    convert_element_type x1 -> x0, other arithmetic: 1.51 us -> none  [body(): back_map = (slot_of[:, None] == slot_ids[None, :]).astype(jnp.bfloat16)]
    reduce_sum x1 -> x0, other arithmetic: 1.45 us -> none  [body(): jnp.sum(jnp.where(slot_of[None, :] == own_slots[:, None], lengths[None, :...]
    pallas_call x1, Pallas kernels: 94.7 us -> 93.5 us  [body(): pl.pallas_call(functools.partial(kernel, (pools, ring, heads, kvh, rows_d...]
where the time goes in v2:
time: 95.3 us; the launch traced here: 95.1 us
  Pallas kernels  93.5 us (98%)
  local copies, waits for them, and re-layouts  1.67 us (2%)
    pallas_call x1, Pallas kernels, body(): pl.pallas_call(functools.partial(kernel, (pools, ring, heads, kvh, rows_d...  93.5 us

profile of v2, /device:TPU:0, one launch (start us, length us, event | category | flops | bytes accessed | tf_op | source)
XLA Modules:
  0.0 95.1 jit_solution(13402637564910709474)
XLA Ops:
  0.0 93.5 %decode_step.1 = bf16[16,8192]{1,0:T(8,128)(2,1)} custom-call(s32[1,256]{1,0:T(1,128)} %bitcast.4, s32[1,256]{1,0:T(1,128)} %bitcast.5, bf16[16,8192]{1,0:T(8,128)(2,1)} %rows_ref.1, f32[1,8192]{1,0:T(1,128)} %bitcast.3, bf16[8192,512]{1,0:T(8,128)(2,1)} %wq_hbm.1, bf16[8192,128]{1,0:T(8,128)(2,1)} %wkv_hbm.1, bf16[512,8192]{1,0:T(8,128)(2,1)} %wo_hbm.1, ...), custom_call_target="tpu_custom_call" | custom-call | tf_op jit(solution)/shard_map/decode_step/pallas_call | solution.py:348
  93.5 1.7 %copy.11 = bf16[16,8192]{1,0:T(8,128)(2,1)} copy(bf16[16,8192]{1,0:T(8,128)(2,1)} %decode_step.1) | data formatting | bytes 524288

commit v3 on v2

--- a/solution.py
+++ b/solution.py
@@ -9,7 +9,7 @@
 
 HD = 128
 EPS = 1e-05
-CHUNKS = 4
+CHUNKS = 2
 SUBS = 4
 TOGETHER = 4
 MESH = pl.DeviceIdType.MESH
@@ -59,15 +59,8 @@
     ]
     barrier = pltpu.get_barrier_semaphore()
 
-    def greet(o, _):
-        peer = lax.rem(me + o, n)
-        pl.semaphore_signal(
-            barrier, inc=1, device_id={"pool": peer // ring, "tensor": lax.rem(peer, ring)},
-            device_id_type=MESH,
-        )
-        return 0
-
-    lax.fori_loop(1, n, greet, 0)
+    for peer in (left, right, other):
+        pl.semaphore_signal(barrier, inc=1, device_id=peer, device_id_type=MESH)
 
     def rows_of(p, t):
         return pl.ds(pl.multiple_of((p * ring + t) * rows_dev, rows_dev), rows_dev)
@@ -75,7 +68,7 @@
     values = rows_ref[...].astype(jnp.float32)
     normed = values * lax.rsqrt(jnp.mean(values * values, axis=1, keepdims=True) + EPS)
     x_buf[rows_of(pool, t_me), :] = (normed * gain_ref[...]).astype(jnp.bfloat16)
-    pl.semaphore_wait(barrier, n - 1)
+    pl.semaphore_wait(barrier, 3)
 
     width = depth // CHUNKS
 

time: 95.3 us -> 92.7 us (0.973)
  Pallas kernels: 93.5 us -> 90.9 us
    pallas_call x1, Pallas kernels: 93.5 us -> 90.9 us  [body(): pl.pallas_call(functools.partial(kernel, (pools, ring, heads, kvh, rows_d...]
where the time goes in v3:
time: 92.7 us; the launch traced here: 92.6 us
  Pallas kernels  90.9 us (98%)
  local copies, waits for them, and re-layouts  1.67 us (2%)
    pallas_call x1, Pallas kernels, body(): pl.pallas_call(functools.partial(kernel, (pools, ring, heads, kvh, rows_d...  90.9 us

profile of v3, /device:TPU:0, one launch (start us, length us, event | category | flops | bytes accessed | tf_op | source)
XLA Modules:
  0.0 92.6 jit_solution(5477682240873870969)
XLA Ops:
  0.0 90.9 %decode_step.1 = bf16[16,8192]{1,0:T(8,128)(2,1)} custom-call(s32[1,256]{1,0:T(1,128)} %bitcast.4, s32[1,256]{1,0:T(1,128)} %bitcast.5, bf16[16,8192]{1,0:T(8,128)(2,1)} %rows_ref.1, f32[1,8192]{1,0:T(1,128)} %bitcast.3, bf16[8192,512]{1,0:T(8,128)(2,1)} %wq_hbm.1, bf16[8192,128]{1,0:T(8,128)(2,1)} %wkv_hbm.1, bf16[512,8192]{1,0:T(8,128)(2,1)} %wo_hbm.1, ...), custom_call_target="tpu_custom_call" | custom-call | tf_op jit(solution)/shard_map/decode_step/pallas_call | solution.py:341
  90.9 1.7 %copy.11 = bf16[16,8192]{1,0:T(8,128)(2,1)} copy(bf16[16,8192]{1,0:T(8,128)(2,1)} %decode_step.1) | data formatting | bytes 524288
